TPU v7x, 32 devices: a whole 2x2x4 slice. The times are simulated.
32 devices in a mesh: lines: 2 (over y), shots: 16 (over z, x, core).
Axes of the slice: x: 2, y: 2, z: 4, core: 2. Of those that a mesh axis runs over, the one named last changes fastest.
Arguments:
- records: bfloat16 [2048, 1024, 256], P(('lines', 'shots')), parts along dimension 0, may hold values from -6 to 6
- missing: int32 [256], P('lines'), parts along dimension 0, may hold values from 0 to 1023, as said below
- neighbours: int32 [256, 3], P('lines'), parts along dimension 0, may hold values from 0 to 1023, as said below
- weights: float32 [256, 3], P('lines'), parts along dimension 0, may hold values from 0.2 to 0.6
- freq_bins: int32 [8], replicated, may hold values from 1 to 127, as said below
Outputs:
- multiples: bfloat16 [2048, 1024, 256], P(('lines', 'shots')), parts along dimension 0
There are 2 independent parts, one for each index of `lines`. A program takes and returns all parts, laid end to end along the dimension named above; an argument that names none is the same for every part. Nothing has to cross between parts.
Inputs may be any that keep to these rules, and one draw needn't show every extreme that they name: `missing`: distinct and ascending; any two missing shots lie 3 or more apart, and every shot within 2 of a missing shot is recorded. `neighbours`: row i names 3 distinct recorded shots, each within 2 of missing[i]. `freq_bins`: 8 distinct bins.
All inputs are finite; a program needn't handle non-finite values.
Results may differ from a plain program's by a relative error of at most 0.0079.
Values may be sent and summed in bfloat16 or wider, within the bound.
A program may use at most 192 MiB of HBM per device.

v0:
```python
import math

import jax
import jax.numpy as jnp
from jax import lax
from jax.sharding import PartitionSpec as P


def from_partner(array, axis, stride):
    return lax.ppermute(array, axis, [(i, i ^ 1 << stride) for i in range(lax.axis_size(axis))])


def tables(freq_bins, sample_count):
    bin_count = freq_bins.shape[0]
    sample_ids = jnp.arange(sample_count, dtype=jnp.int32)
    phases = freq_bins[None, :] * sample_ids[:, None] % sample_count
    angles = phases.astype(jnp.float32) * (2.0 * math.pi / sample_count)
    trig_pair = jnp.stack([jnp.cos(angles), -jnp.sin(angles)], axis=-1)
    forward = (trig_pair / math.sqrt(sample_count)).astype(jnp.bfloat16)
    inverse = (trig_pair * math.sqrt(2.0 / bin_count)).astype(jnp.bfloat16)
    return (forward, inverse)


def add_block(summed, right_source, block_piece, source_part, width):
    right_rows = lax.dynamic_slice_in_dim(right_source, source_part * width, width, 2)
    right_real = right_rows[:, 0]
    right_imag = right_rows[:, 1]
    left_side = jnp.concatenate([block_piece[:, 0], block_piece[:, 1]], axis=-1)
    right_side = jnp.concatenate(
        [
            jnp.concatenate([right_real, right_imag], axis=-1),
            jnp.concatenate([-right_imag, right_real], axis=-1),
        ],
        axis=1,
    )
    return summed + jnp.einsum(
        "zsk,zkc->zsc", left_side, right_side, preferred_element_type=jnp.float32
    )


def shards(records, missing, neighbours, weights, freq_bins):
    devices = lax.axis_size("shots")
    position = lax.axis_index("shots")
    shot_rows = records.shape[0]
    matrix_order = records.shape[1]
    sample_count = records.shape[2]
    half = matrix_order // 2
    couples = devices // 2
    neigh_count = neighbours.shape[1]
    forward, inverse = tables(freq_bins, sample_count)
    blocked = records.reshape(shot_rows, 2, half, sample_count)
    spectra = jnp.einsum(
        "shrt,tpc->phcsr", blocked, forward, preferred_element_type=jnp.float32
    ).astype(jnp.bfloat16)
    outgoing = spectra.reshape(devices, 2, shot_rows, half)
    incoming = lax.all_to_all(outgoing, "shots", split_axis=0, concat_axis=2, tiled=True)
    own_block = incoming
    filled_rows = jnp.zeros(
        own_block.shape[:2] + (missing.shape[0], own_block.shape[3]), jnp.float32
    )
    for slot_index in range(neigh_count):
        picked = jnp.take(own_block, neighbours[:, slot_index], axis=2)
        filled_rows = filled_rows + weights[:, slot_index][:, None] * picked.astype(jnp.float32)
    own_block = own_block.at[:, :, missing, :].set(filled_rows.astype(jnp.bfloat16))
    factor = -1.0 / math.sqrt(matrix_order)
    member = position % 2
    other_half = from_partner(own_block, "shots", 0)
    summed = jnp.zeros((1, matrix_order, 2 * half), jnp.float32)
    summed = add_block(summed, own_block, own_block, member, half)
    summed = add_block(summed, own_block, other_half, 1 - member, half)
    predicted = (summed * factor).astype(jnp.bfloat16)
    outgoing_back = predicted.reshape(1, 1, matrix_order, 2, half)
    returned = lax.all_to_all(outgoing_back, "shots", split_axis=2, concat_axis=0, tiled=True)
    returned = returned.reshape(couples, 2, shot_rows, 2, half)
    inverse_pair = jnp.transpose(inverse, (1, 2, 0))
    multiples = jnp.einsum(
        "phsir,pit->shrt", returned, inverse_pair, preferred_element_type=jnp.float32
    )
    return multiples.astype(jnp.bfloat16).reshape(shot_rows, matrix_order, sample_count)


def solution(mesh):
    return jax.shard_map(
        shards,
        mesh=mesh,
        in_specs=(
            P(("lines", "shots"), None, None),
            P("lines"),
            P("lines", None),
            P("lines", None),
            P(),
        ),
        out_specs=P(("lines", "shots"), None, None),
        check_vma=False,
    )
```

profile of v0, /device:TPU:15, one launch (start us, length us, event | category | flops | bytes accessed | tf_op | source)
XLA Modules:
  0.0 225.0 jit_solution(15952306101126947677)
XLA Ops:
  0.0 0.8 fusion.33
  0.8 14.2 %convert_bitcast_fusion = bf16[8,2,2,64,512]{4,0,1,3,2:T(8,128)(2,1)S(1)} fusion(bf16[64,2,512,256,1]{3,2,1,0,4:T(8,128)(2,1)} %bitcast.127, f32[256,8,1]{0,1,2:T(8,128)S(1)} %get-tuple-element.30, f32[256,8,1]{0,1,2:T(8,128)S(1)} %get-tuple-element.29), kind=kOutput, calls=%fused_computation.31 | convolution fusion | flops 537931776 | bytes 35667968 | tf_op jit(solution)/shard_map/shrt,tpc->phcsr/dot_general | solution.py:52
  15.0 2.5 %copy.40 = bf16[8,2,2,64,512]{4,3,2,1,0:T(8,128)(2,1)} copy(bf16[8,2,2,64,512]{4,0,1,3,2:T(8,128)(2,1)S(1)} %convert_bitcast_fusion) | data formatting | bytes 4194304 | tf_op jit(solution)/shard_map/convert_element_type | solution.py:54
  17.5 0.0 copy-start.3
  17.5 0.0 copy-start.4
  17.5 0.0 copy-start.2
  17.5 6.7 %all-to-all-start = ((bf16[16,2,64,512]{3,2,1,0:T(8,128)(2,1)}), bf16[16,2,64,512]{3,2,1,0:T(8,128)(2,1)S(1)}, u32[]{:S(2)}, u32[]{:S(2)}) async-start(bf16[16,2,64,512]{3,2,1,0:T(8,128)(2,1)} %bitcast.131), calls=%async_computation | async-start | bytes 4194304 | tf_op jit(solution)/shard_map/all_to_all | solution.py:56
  24.2 0.0 copy-done.3
  24.2 0.0 copy-done.4
  24.2 0.0 copy-done.2
  24.3 47.3 %all-to-all-done = bf16[16,2,64,512]{3,2,1,0:T(8,128)(2,1)S(1)} async-done(((bf16[16,2,64,512]{3,2,1,0:T(8,128)(2,1)}), bf16[16,2,64,512]{3,2,1,0:T(8,128)(2,1)S(1)}, u32[]{:S(2)}, u32[]{:S(2)}) %all-to-all-start) | async-done | bytes 2097184 | tf_op jit(solution)/shard_map/all_to_all | solution.py:56
  71.6 0.0 copy-start
  71.6 1.3 copy-done
  72.9 0.0 copy-start.1
  72.9 3.9 %copy.41 = bf16[1,2,16,64,512]{4,1,3,2,0:T(2,128)(2,1)S(1)} copy(bf16[1,2,16,64,512]{4,3,1,2,0:T(8,128)(2,1)} %bitcast.128) | data formatting | bytes 4194304 | tf_op jit(solution)/shard_map/all_to_all | solution.py:56
  76.8 0.0 copy-done.1
  76.8 0.2 copy.42
  77.0 3.5 %copy.77 = bf16[1,2,1024,512]{3,1,2,0:T(2,128)(2,1)} copy(bf16[1,2,1024,512]{3,2,1,0:T(8,128)(2,1)S(1)} %bitcast.132) | data formatting | bytes 4194304 | tf_op jit(solution)/shard_map/all_to_all | solution.py:56
  80.5 2.7 %gather_fusion.2 = bf16[128,2,512]{2,1,0:T(2,128)(2,1)S(1)} fusion(bf16[2,1024,512]{2,0,1:T(2,128)(2,1)} %bitcast.137, s32[1024]{0:T(1024)S(1)} %get-tuple-element.31), kind=kCustom, calls=%fused_computation.2.clone | custom fusion | bytes 524800 | tf_op jit(solution)/shard_map/jit(_take)/gather | solution.py:62
  83.2 2.7 %gather_fusion.1 = bf16[128,2,512]{2,1,0:T(2,128)(2,1)S(1)} fusion(bf16[2,1024,512]{2,0,1:T(2,128)(2,1)} %bitcast.138, s32[1024]{0:T(1024)S(1)} %get-tuple-element.32), kind=kCustom, calls=%fused_computation.1.clone | custom fusion | bytes 524800 | tf_op jit(solution)/shard_map/jit(_take)/gather | solution.py:62
  86.0 2.7 %gather_fusion = bf16[128,2,512]{2,1,0:T(2,128)(2,1)S(1)} fusion(bf16[2,1024,512]{2,0,1:T(2,128)(2,1)} %bitcast.139, s32[1024]{0:T(1024)S(1)} %pad_clamp_fusion.2), kind=kCustom, calls=%fused_computation.clone | custom fusion | bytes 524800 | tf_op jit(solution)/shard_map/jit(_take)/gather | solution.py:62
  88.7 0.3 fusion.20
  89.0 0.3 copy.49
  89.3 4.4 %scatter_fusion = bf16[2,1024,512]{2,0,1:T(2,128)(2,1)S(1)} fusion(bf16[2,1024,512]{2,0,1:T(2,128)(2,1)S(1)} %bitcast.124, s32[128]{0:T(128)S(1)} %compare_select_fusion.3, bf16[128,2,512]{2,1,0:T(2,128)(2,1)S(1)} %copy.49), kind=kCustom, calls=%fused_computation.3 | custom fusion | bytes 786944 | tf_op jit(solution)/shard_map/scatter | solution.py:64
  93.7 1.4 constant_dynamic-slice_fusion
  95.1 0.2 copy.82
  95.3 0.2 copy.83
  95.5 0.3 collective-permute-start
  95.7 3.2 %fusion.43 = (bf16[1,1,1024,512]{3,1,2,0:T(2,128)(2,1)S(1)}, bf16[1,1,1024,512]{3,1,2,0:T(2,128)(2,1)S(1)}) fusion(bf16[1,2,1024,512]{3,1,2,0:T(2,128)(2,1)S(1)} %bitcast.126), kind=kLoop, calls=%fused_computation.89 | loop fusion | bytes 4194304 | tf_op jit(solution)/shard_map/slice | solution.py:28
  98.9 0.3 copy.81
  99.2 0.3 copy.80
  99.6 0.1 slice_bitcast_fusion
  99.7 0.1 slice_bitcast_fusion.2
  99.8 2.5 %fusion.1 = f32[1024,1024]{0,1:T(8,128)S(1)} fusion(bf16[1,1024,512]{2,1,0:T(8,128)(2,1)S(1)} %bitcast.142, bf16[1,1024,512]{2,1,0:T(8,128)(2,1)S(1)} %bitcast.141, bf16[1,512,512]{2,1,0:T(8,128)(2,1)S(1)} %get-tuple-element.21, bf16[1,512,512]{2,1,0:T(8,128)(2,1)S(1)} %fusion.40, bf16[1,512,512]{2,1,0:T(8,128)(2,1)S(1)} %get-tuple-element.20), kind=kOutput, calls=%fused_computation.8 | convolution fusion | flops 2160066560 | bytes 7864320 | tf_op jit(solution)/shard_map/zsk,zkc->zsc/dot_general | solution.py:36
  102.2 0.0 collective-permute-done
  102.2 3.0 %fusion.42 = (bf16[1,1,1024,512]{3,1,2,0:T(2,128)(2,1)S(1)}, bf16[1,1,1024,512]{3,1,2,0:T(2,128)(2,1)S(1)}) fusion(bf16[1,2,1024,512]{3,1,2,0:T(2,128)(2,1)S(1)} %collective-permute-done), kind=kLoop, calls=%fused_computation.88 | loop fusion | bytes 4194304 | tf_op jit(solution)/shard_map/slice | solution.py:28
  105.2 0.3 copy.79
  105.5 0.3 copy.78
  105.8 4.0 %multiply_convert_fusion = bf16[1024,1024]{0,1:T(8,128)(2,1)} fusion(f32[1024,1024]{0,1:T(8,128)S(1)} %fusion.1, bf16[1,512,512]{2,1,0:T(8,128)(2,1)S(1)} %get-tuple-element.19, bf16[1,512,512]{2,1,0:T(8,128)(2,1)S(1)} %fusion.41, bf16[1,512,512]{2,1,0:T(8,128)(2,1)S(1)} %get-tuple-element.18, bf16[1,1024,512]{2,1,0:T(8,128)(2,1)S(1)} %bitcast.144, ...), kind=kOutput, calls=%fused_computation.6 | convolution fusion | flops 2163212288 | bytes 9961472 | tf_op jit(solution)/shard_map/zsk,zkc->zsc/dot_general | solution.py:36
  109.8 4.8 %copy.52 = bf16[1,1,1024,2,512]{4,3,1,0,2:T(2,128)(2,1)S(1)} copy(bf16[1,1,1024,2,512]{2,4,3,1,0:T(8,128)(2,1)} %bitcast.140) | data formatting | bytes 4194304 | tf_op jit(solution)/shard_map/reshape | solution.py:72
  114.6 52.1 %all_to_all.27 = bf16[1,1,1024,2,512]{4,3,1,0,2:T(2,128)(2,1)S(1)} all-to-all(bf16[1,1,1024,2,512]{4,3,1,0,2:T(2,128)(2,1)S(1)} %copy.52), channel_id=1, replica_groups=mesh['lines'=2,'shots'=16] {'shots'}, dimensions={2} | all-to-all | bytes 4194304 | tf_op jit(solution)/shard_map/all_to_all | solution.py:73
  166.7 14.1 %fusion = bf16[64,2,512,256]{2,3,0,1:T(8,128)(2,1)} fusion(bf16[8,2,64,2,512]{4,3,2,1,0:T(2,128)(2,1)S(1)} %bitcast.130, f32[256,8,1]{0,1,2:T(8,128)S(1)} %get-tuple-element.30, f32[256,8,1]{0,1,2:T(8,128)S(1)} %get-tuple-element.29), kind=kOutput, calls=%fused_computation.5 | convolution fusion | flops 553660416 | bytes 35667968 | tf_op jit(solution)/shard_map/phsir,pit->shrt/dot_general | solution.py:76
  180.8 44.2 %copy.55 = bf16[64,2,512,256]{3,2,1,0:T(8,128)(2,1)} copy(bf16[64,2,512,256]{2,3,0,1:T(8,128)(2,1)} %fusion) | data formatting | bytes 67108864 | tf_op jit(solution)/shard_map/convert_element_type | solution.py:79
  (7 shorter events, 0.1 us)
Async XLA Ops:
  17.5 6.7 %copy-start.3 = (s32[128,3]{0,1:T(4,128)S(1)}, s32[128,3]{0,1:T(4,128)}, u32[]{:S(2)}) copy-start(s32[128,3]{0,1:T(4,128)} %param.9) | copy-start | bytes 4612
  17.5 6.7 %copy-start.4 = (s32[128]{0:T(128)S(1)}, s32[128]{0:T(128)}, u32[]{:S(2)}) copy-start(s32[128]{0:T(128)} %param.8) | copy-start | bytes 1540
  17.5 6.8 %copy-start.2 = (f32[128,3]{0,1:T(4,128)S(1)}, f32[128,3]{0,1:T(4,128)}, u32[]{:S(2)}) copy-start(f32[128,3]{0,1:T(4,128)} %param.10) | copy-start | bytes 4612
  17.5 54.1 %all-to-all-start = ((bf16[16,2,64,512]{3,2,1,0:T(8,128)(2,1)}), bf16[16,2,64,512]{3,2,1,0:T(8,128)(2,1)S(1)}, u32[]{:S(2)}, u32[]{:S(2)}) async-start(bf16[16,2,64,512]{3,2,1,0:T(8,128)(2,1)} %bitcast.131), calls=%async_computation | async-start | bytes 4194304 | tf_op jit(solution)/shard_map/all_to_all | solution.py:56
  71.6 1.3 copy-start
  72.9 3.9 %copy-start.1 = (bf16[16,2,64,512]{3,2,1,0:T(8,128)(2,1)S(1)}, bf16[16,2,64,512]{3,2,1,0:T(8,128)(2,1)}, u32[]{:S(2)}) copy-start(bf16[16,2,64,512]{3,2,1,0:T(8,128)(2,1)} %copy-done) | copy-start | bytes 6291460
  95.5 6.8 %collective-permute-start = (bf16[1,2,1024,512]{3,1,2,0:T(2,128)(2,1)S(1)}, bf16[1,2,1024,512]{3,1,2,0:T(2,128)(2,1)S(1)}, u32[]{:S(2)}, u32[]{:S(2)}) collective-permute-start(bf16[1,2,1024,512]{3,1,2,0:T(2,128)(2,1)S(1)} %bitcast.125), channel_id=1, source_target_pairs={{0,1},{1,0},{2,3},{3,2},{4,5},{5,4},{6,7},{7,6},{8,9},{9,8},{10,11... | collective-permute-start | bytes 6291464 | tf_op jit(solution)/shard_map/ppermute | solution.py:10
where the time goes:
time: 228 us; the launch traced here: 225 us
  local copies, waits for them, and re-layouts  82.5 us (36%)
  blocking collectives  52.1 us (23%)
  waiting for transfers between devices  47.3 us (21%)
  matrix products  34.7 us (15%)
  starting transfers between devices  6.96 us (3%)
    all_to_all x1, blocking collectives, shards(): lax.all_to_all(outgoing_back, 'shots', split_axis=2, concat_axis=0, tiled...  52.1 us
    all_to_all x1, waiting for transfers between devices, shards(): lax.all_to_all(outgoing, 'shots', split_axis=0, concat_axis=2, tiled=True)  47.3 us
    convert_element_type x1, local copies, waits for them, and re-layouts, shards(): multiples.astype(jnp.bfloat16)  44.2 us
    dot_general x1, matrix products, shards(): jnp.einsum('shrt,tpc->phcsr', blocked, forward, preferred_element_type=jn...  14.2 us
    dot_general x1, matrix products, shards(): jnp.einsum('phsir,pit->shrt', returned, inverse_pair, preferred_element_t...  14.1 us
    gather x3, local copies, waits for them, and re-layouts, shards(): picked = jnp.take(own_block, neighbours[:, slot_index], axis=2)  8.18 us
    all_to_all x3, local copies, waits for them, and re-layouts, shards(): lax.all_to_all(outgoing, 'shots', split_axis=0, concat_axis=2, tiled=True)  7.59 us
    all_to_all x1, starting transfers between devices, shards(): lax.all_to_all(outgoing, 'shots', split_axis=0, concat_axis=2, tiled=True)  6.69 us
  transfers between devices with their start and end apart: 2, of which 1 were waited for; matrix products, arithmetic and copies ran while one was open for 3% of the time, Pallas kernels for 0%

commit v1 on v0

v1 whole, which is shorter than its diff:
```python
import functools
import math

import jax
import jax.numpy as jnp
from jax import lax
from jax.experimental import pallas as pl
from jax.experimental.pallas import tpu as pltpu
from jax.sharding import PartitionSpec as P

SB = 16
MESH = pl.DeviceIdType.MESH


def tables(freq_bins, sample_count):
    bin_count = freq_bins.shape[0]
    sample_ids = jnp.arange(sample_count, dtype=jnp.int32)
    phases = freq_bins[:, None] * sample_ids[None, :] % sample_count
    angles = phases.astype(jnp.float32) * (2.0 * math.pi / sample_count)
    trig_pair = jnp.stack([jnp.cos(angles), -jnp.sin(angles)], axis=1)
    forward = (trig_pair / math.sqrt(sample_count)).astype(jnp.bfloat16)
    inverse = (trig_pair * math.sqrt(2.0 / bin_count)).astype(jnp.bfloat16)
    return (forward, inverse)


def fill_rows(missing, neighbours, weights, rows, cols):
    hit = missing[None, :] == rows.reshape(-1, 1)
    kept = jnp.logical_not(jnp.any(hit, axis=1)).reshape(rows.shape)
    out = jnp.where((rows == cols) & kept, 1.0, 0.0)
    for k in range(neighbours.shape[1]):
        w = jnp.sum(jnp.where(hit, weights[None, :, k], 0.0), axis=1).reshape(rows.shape)
        n = jnp.sum(jnp.where(hit, neighbours[None, :, k], 0), axis=1).reshape(rows.shape)
        out = out + jnp.where(n == cols, w, 0.0)
    return out.astype(jnp.bfloat16)


def row_mod(shape):
    return lax.broadcasted_iota(jnp.int32, shape, 0) % SB


def main_kernel(
    n, bins, rows, half, blocks,
    x_ref, base_ref, gb_ref, back_ref,
    send, recv, other, full, right, ret,
    send_sem, recv_sem, fsend, frecv, bsend, brecv, lsem,
):
    step = pl.program_id(0) * 2 + pl.program_id(1)
    sb, h = pl.program_id(0), pl.program_id(1)
    me = lax.axis_index("shots")
    member = me % 2
    mine = me // 2
    order = n * rows

    @pl.when(step == 0)
    def _():
        barrier = pltpu.get_barrier_semaphore()

        def greet(d, c):
            pl.semaphore_signal(
                barrier, inc=1, device_id={"shots": (me + d) % n}, device_id_type=MESH
            )
            return c

        lax.fori_loop(1, n, greet, 0)
        pl.semaphore_wait(barrier, n - 1)

    mod = row_mod((bins * 2 * SB, x_ref.shape[2]))
    base = base_ref[...]
    acc = jnp.zeros((bins * 2 * SB, half), jnp.float32)
    for s in range(SB):
        left = jnp.where(mod == s, base, jnp.zeros_like(base))
        acc = acc + lax.dot_general(
            left, x_ref[s], (((1,), (1,)), ((), ())), preferred_element_type=jnp.float32
        )
    at = pl.multiple_of(sb * SB, SB)
    send[:, h, :, pl.ds(at, SB), :] = acc.astype(jnp.bfloat16).reshape(bins, 2, SB, half)

    def out_copy(j, hh, sbb):
        a = pl.multiple_of(sbb * SB, SB)
        return pltpu.make_async_remote_copy(
            src_ref=send.at[j, hh, :, pl.ds(a, SB), :],
            dst_ref=recv.at[me, :, pl.ds(a, SB), :],
            send_sem=send_sem.at[j * 2 + hh, sbb],
            recv_sem=recv_sem.at[me, sbb],
            device_id={"shots": j * 2 + hh},
            device_id_type=MESH,
        )

    def start_out(d, c):
        j = (mine + d) % bins

        @pl.when(j * 2 + h != me)
        def _():
            out_copy(j, h, sb).start()

        return c

    lax.fori_loop(1, bins + 1, start_out, 0)

    @pl.when(h == member)
    def _():
        recv[me, :, pl.ds(at, SB), :] = send[mine, h, :, pl.ds(at, SB), :]

    @pl.when(step == 2 * blocks - 1)
    def _():
        sibling = mine * 2 + 1 - member

        def forward(p, sbb):
            a = pl.multiple_of(sbb * SB, SB)
            return pltpu.make_async_remote_copy(
                src_ref=recv.at[p, :, pl.ds(a, SB), :],
                dst_ref=other.at[p, :, pl.ds(a, SB), :],
                send_sem=fsend.at[p, sbb],
                recv_sem=frecv.at[p, sbb],
                device_id={"shots": sibling},
                device_id_type=MESH,
            )

        def arrive(i, c):
            sbb, p = i // n, (me + i) % n
            a = pl.multiple_of(sbb * SB, SB)

            @pl.when(p != me)
            def _():
                pltpu.make_async_remote_copy(
                    src_ref=recv.at[p, :, pl.ds(a, SB), :],
                    dst_ref=recv.at[p, :, pl.ds(a, SB), :],
                    send_sem=send_sem.at[p, sbb],
                    recv_sem=recv_sem.at[p, sbb],
                    device_id={"shots": sibling},
                    device_id_type=MESH,
                ).wait_recv()

            forward(p, sbb).start()
            return c

        lax.fori_loop(0, blocks * n, arrive, 0)

        def fill(src, keep):
            def one(b, c):
                first = jnp.minimum(jnp.maximum(2 * b - 1, 0), n - 4)
                g = gb_ref[b]
                at_row = pl.multiple_of(b * 2 * rows, 2 * rows)
                for ch in range(2):
                    piece = src[pl.ds(first, 4), ch].reshape(4 * rows, half)
                    val = jnp.dot(g, piece, preferred_element_type=jnp.float32)
                    keep(ch, at_row, val.astype(jnp.bfloat16))
                return c

            lax.fori_loop(0, n // 2, one, 0)

        def keep_own(ch, at_row, val):
            full[ch, member, pl.ds(at_row, 2 * rows), :] = val
            right[ch, pl.ds(at_row, 2 * rows), :] = val
            if ch == 1:
                right[2, pl.ds(at_row, 2 * rows), :] = -val

        def keep_other(ch, at_row, val):
            full[ch, 1 - member, pl.ds(at_row, 2 * rows), :] = val

        fill(recv, keep_own)

        def arrived(i, c):
            forward(i % n, i // n).wait()
            return c

        lax.fori_loop(0, blocks * n, arrived, 0)
        fill(other, keep_other)

        def back_copy(p):
            return pltpu.make_async_remote_copy(
                src_ref=ret.at[p],
                dst_ref=back_ref.at[me],
                send_sem=bsend.at[p],
                recv_sem=brecv.at[me],
                device_id={"shots": p},
                device_id_type=MESH,
            )

        own_back = pltpu.make_async_copy(ret.at[me], back_ref.at[me], lsem)
        factor = -1.0 / math.sqrt(order)
        groups = n // 4
        wide = 256

        def product(i, c):
            g = (me // 4 + groups // 2 + i) % groups
            at_row = pl.multiple_of(g * 4 * rows, 4 * rows)

            for col in range(0, half, wide):
                for ch in range(2):
                    out = None
                    for m in range(2):
                        for lc in range(2):
                            rc = (0 if lc == 0 else 2) if ch == 0 else (1 if lc == 0 else 0)
                            term = jnp.dot(
                                full[lc, m, pl.ds(at_row, 4 * rows), :],
                                right[rc, m * half:(m + 1) * half, col:col + wide],
                                preferred_element_type=jnp.float32,
                            )
                            out = term if out is None else out + term
                    ret[pl.ds(4 * g, 4), ch, :, col:col + wide] = (
                        (out * factor).astype(jnp.bfloat16).reshape(4, rows, wide)
                    )

            def post(q, c2):
                p = 4 * g + q

                @pl.when(p != me)
                def _():
                    back_copy(p).start()

                @pl.when(p == me)
                def _():
                    own_back.start()

                return c2

            lax.fori_loop(0, 4, post, 0)
            return c

        lax.fori_loop(0, groups, product, 0)
        own_back.wait()

        def sent(i, c):
            sbb, p = i // n, i % n

            @pl.when(p != me)
            def _():
                out_copy(p // 2, p % 2, sbb).wait_send()

            return c

        lax.fori_loop(0, blocks * n, sent, 0)

        def finish(p, c):
            @pl.when(p != me)
            def _():
                back_copy(p).wait_send()
                pltpu.make_async_remote_copy(
                    src_ref=ret.at[p],
                    dst_ref=back_ref.at[p],
                    send_sem=bsend.at[p],
                    recv_sem=brecv.at[p],
                    device_id={"shots": p},
                    device_id_type=MESH,
                ).wait_recv()

            return c

        lax.fori_loop(0, n, finish, 0)


def inverse_kernel(p_ref, base_ref, o_ref):
    bins, half = p_ref.shape[0], p_ref.shape[-1]
    block = p_ref[...].reshape(bins * 2 * SB, half)
    turned = block.T
    base = base_ref[...]
    mod = row_mod(base.shape)
    for s in range(SB):
        rhs = jnp.where(mod == s, base, jnp.zeros_like(base))
        o_ref[s] = jnp.dot(turned, rhs, preferred_element_type=jnp.float32).astype(jnp.bfloat16)


def fused(records, missing, neighbours, weights, freq_bins):
    n = lax.axis_size("shots")
    rows, order, samples = records.shape
    half = order // 2
    bins = freq_bins.shape[0]
    blocks = rows // SB
    forward, inverse = tables(freq_bins, samples)
    forward = jnp.repeat(forward.reshape(2 * bins, samples), SB, axis=0)
    inverse = jnp.repeat(inverse.reshape(2 * bins, samples), SB, axis=0)
    b = jnp.arange(n // 2, dtype=jnp.int32)
    first = jnp.clip(2 * b - 1, 0, n - 4) * rows
    gshape = (n // 2, 2 * rows, 4 * rows)
    row_ids = (b[:, None] * 2 * rows + jnp.arange(2 * rows, dtype=jnp.int32)[None, :])[:, :, None]
    col_ids = (first[:, None] + jnp.arange(4 * rows, dtype=jnp.int32)[None, :])[:, None, :]
    gb = fill_rows(missing, neighbours, weights, row_ids, col_ids)
    assert gb.shape == gshape
    cut = bins * 2 * SB
    bf16 = jnp.bfloat16
    dma = pltpu.SemaphoreType.DMA
    back = pl.pallas_call(
        functools.partial(main_kernel, n, bins, rows, half, blocks),
        grid=(blocks, 2),
        out_shape=jax.ShapeDtypeStruct((n, 2, rows, half), bf16),
        in_specs=[
            pl.BlockSpec((SB, half, samples), lambda i, j: (i, j, 0)),
            pl.BlockSpec((cut, samples), lambda i, j: (0, 0)),
            pl.BlockSpec(gshape, lambda i, j: (0, 0, 0)),
        ],
        out_specs=pl.BlockSpec(memory_space=pl.ANY),
        scratch_shapes=[
            pltpu.VMEM((bins, 2, 2, rows, half), bf16),
            pltpu.VMEM((n, 2, rows, half), bf16),
            pltpu.VMEM((n, 2, rows, half), bf16),
            pltpu.VMEM((2, 2, order, half), bf16),
            pltpu.VMEM((3, order, half), bf16),
            pltpu.VMEM((n, 2, rows, half), bf16),
            dma((n, blocks)),
            dma((n, blocks)),
            dma((n, blocks)),
            dma((n, blocks)),
            dma((n,)),
            dma((n,)),
            dma,
        ],
        compiler_params=pltpu.CompilerParams(
            collective_id=0, has_side_effects=True, vmem_limit_bytes=50 * 2**20
        ),
    )(records, forward, gb)
    back = back.reshape(bins, 2, 2, rows, half)
    return pl.pallas_call(
        inverse_kernel,
        grid=(blocks, 2),
        out_shape=jax.ShapeDtypeStruct(records.shape, bf16),
        in_specs=[
            pl.BlockSpec((bins, None, 2, SB, half), lambda i, j: (0, j, 0, i, 0)),
            pl.BlockSpec((cut, samples), lambda i, j: (0, 0)),
        ],
        out_specs=pl.BlockSpec((SB, half, samples), lambda i, j: (i, j, 0)),
        compiler_params=pltpu.CompilerParams(vmem_limit_bytes=50 * 2**20),
    )(back, inverse)


def plain(records, missing, neighbours, weights, freq_bins):
    devices = lax.axis_size("shots")
    position = lax.axis_index("shots")
    shot_rows, order, sample_count = records.shape
    half = order // 2
    couples = devices // 2
    forward, inverse = tables(freq_bins, sample_count)
    blocked = records.reshape(shot_rows, 2, half, sample_count)
    spectra = jnp.einsum(
        "shrt,pct->phcsr", blocked, forward, preferred_element_type=jnp.float32
    ).astype(jnp.bfloat16)
    outgoing = spectra.reshape(devices, 2, shot_rows, half)
    own = lax.all_to_all(outgoing, "shots", split_axis=0, concat_axis=2, tiled=True)[0]
    ids = jnp.arange(order, dtype=jnp.int32)
    g = fill_rows(missing, neighbours, weights, ids[:, None], ids[None, :])
    own = jnp.einsum("st,ctr->csr", g, own, preferred_element_type=jnp.float32)
    own = own.astype(jnp.bfloat16)
    member = position % 2
    other = lax.ppermute(own, "shots", [(i, i ^ 1) for i in range(devices)])
    real, imag = 0.0, 0.0
    for left, part in ((own, member), (other, 1 - member)):
        right = lax.dynamic_slice_in_dim(own, part * half, half, 1)
        dot = functools.partial(jnp.dot, preferred_element_type=jnp.float32)
        real = real + dot(left[0], right[0]) - dot(left[1], right[1])
        imag = imag + dot(left[0], right[1]) + dot(left[1], right[0])
    predicted = (jnp.stack([real, imag]) * (-1.0 / math.sqrt(order))).astype(jnp.bfloat16)
    outgoing = predicted.reshape(2, devices, shot_rows, half)
    outgoing = jnp.transpose(outgoing, (1, 0, 2, 3))
    returned = lax.all_to_all(outgoing, "shots", split_axis=0, concat_axis=0, tiled=True)
    returned = returned.reshape(couples, 2, 2, shot_rows, half)
    multiples = jnp.einsum(
        "phcsr,pct->shrt", returned, inverse, preferred_element_type=jnp.float32
    )
    return multiples.astype(jnp.bfloat16).reshape(shot_rows, order, sample_count)


def shards(records, missing, neighbours, weights, freq_bins):
    n = lax.axis_size("shots")
    rows, order, samples = records.shape
    bins = freq_bins.shape[0]
    fits = (
        rows % SB == 0 and n % 4 == 0 and n >= 8 and n == 2 * bins and order == n * rows
        and order % 512 == 0 and rows >= 2 and bins <= 8
    )
    return (fused if fits else plain)(records, missing, neighbours, weights, freq_bins)


def solution(mesh):
    return jax.shard_map(
        shards,
        mesh=mesh,
        in_specs=(
            P(("lines", "shots"), None, None),
            P("lines"),
            P("lines", None),
            P("lines", None),
            P(),
        ),
        out_specs=P(("lines", "shots"), None, None),
        check_vma=False,
    )
```

time: 228 us -> 130 us (0.57); the launches traced: 225 us -> 130 us
  Pallas kernels: 0 us -> 122 us
  local copies, waits for them, and re-layouts: 82.5 us -> 1.66 us
  blocking collectives: 52.1 us -> 0 us
  waiting for transfers between devices: 47.3 us -> 0 us
  matrix products: 34.7 us -> 0 us
  starting transfers between devices: 6.96 us -> 0 us
  other arithmetic: 1.16 us -> 5.97 us
    pallas_call x0 -> x2, Pallas kernels: none -> 122 us  [the longest x1 107 us: fused(): pl.pallas_call(functools.partial(main_kernel, n, bins, rows, half, blocks...]
    all_to_all x1 -> x0, blocking collectives: 52.1 us -> none  [shards(): lax.all_to_all(outgoing_back, 'shots', split_axis=2, concat_axis=0, tiled...]
    all_to_all x1 -> x0, waiting for transfers between devices: 47.3 us -> none  [shards(): lax.all_to_all(outgoing, 'shots', split_axis=0, concat_axis=2, tiled=True)]
    convert_element_type x3 -> x4, local copies, waits for them, and re-layouts: 47 us -> 0.04 us  [the longest x2 0.02 us: tables(): forward = (trig_pair / math.sqrt(sample_count)).astype(jnp.bfloat16)]
    dot_general x4 -> x0, matrix products: 34.7 us -> none  [the longest x1 14.2 us: shards(): jnp.einsum('shrt,tpc->phcsr', blocked, forward, preferred_element_type=jn...]
    gather x3 -> x0, local copies, waits for them, and re-layouts: 8.18 us -> none  [shards(): picked = jnp.take(own_block, neighbours[:, slot_index], axis=2)]
    all_to_all x3 -> x0, local copies, waits for them, and re-layouts: 7.59 us -> none  [shards(): lax.all_to_all(outgoing, 'shots', split_axis=0, concat_axis=2, tiled=True)]
    all_to_all x1 -> x0, starting transfers between devices: 6.69 us -> none  [shards(): lax.all_to_all(outgoing, 'shots', split_axis=0, concat_axis=2, tiled=True)]
  transfers between devices with their start and end apart: 2 -> 0, of which waited for: 1 -> 0; matrix products, arithmetic and copies ran while one was open for 3% -> 0% of each run, Pallas kernels for 0% -> 0%
where the time goes in v1:
time: 130 us
  Pallas kernels  122 us (94%)
  other arithmetic  5.97 us (5%)
  local copies, waits for them, and re-layouts  1.66 us (1%)
    pallas_call x1, Pallas kernels, fused(): pl.pallas_call(functools.partial(main_kernel, n, bins, rows, half, blocks...  107 us
    pallas_call x1, Pallas kernels, fused(): pl.pallas_call(inverse_kernel, grid=(blocks, 2), out_shape=jax.ShapeDtype...  14.7 us

profile of v1, /device:TPU:15, one launch (start us, length us, event | category | flops | bytes accessed | tf_op | source)
XLA Modules:
  0.0 129.5 jit_solution(5030794928745627944)
XLA Ops:
  0.0 0.8 slice_bitcast_fusion.3
  0.8 0.8 slice_bitcast_fusion.2
  1.6 0.1 iota_add_fusion
  1.7 0.1 iota_add_fusion.1
  1.7 1.0 compare_reduce_fusion
  2.8 1.3 fusion.1
  4.1 1.3 fusion
  5.4 0.8 fusion.12
  6.3 1.4 %add_convert_fusion.gb_ref = bf16[8,128,256]{2,1,0:T(8,128)(2,1)S(1)} fusion(f32[8,128]{1,0:T(8,128)S(1)} %bitcast.29, s32[8,128]{1,0:T(8,128)S(1)} %bitcast.32, f32[8,128]{1,0:T(8,128)S(1)} %bitcast.30, s32[8,128]{1,0:T(8,128)S(1)} %bitcast.33, f32[8,128]{1,0:T(8,128)S(1)} %bitcast.28, s32[8,128]{1,0:T(8,128)S(1)} %bitcast.31, ...), kind=kLoop, calls=%fused_computation.7 | loop fusion | flops 3407872 | bytes 562176 | tf_op jit(solution)/shard_map/convert_element_type | solution.py:34
  7.7 107.1 %shard_map.55 = bf16[16,2,64,512]{3,2,1,0:T(8,128)(2,1)S(1)} custom-call(bf16[64,1024,256]{2,1,0:T(8,128)(2,1)} %x_ref.1, bf16[256,256]{1,0:T(8,128)(2,1)S(1)} %bitcast.27, bf16[8,128,256]{2,1,0:T(8,128)(2,1)S(1)} %add_convert_fusion.gb_ref), custom_call_target="tpu_custom_call" | custom-call | tf_op jit(solution)/shard_map/pallas_call | solution.py:283
  114.8 14.7 %shard_map.56 = bf16[64,1024,256]{2,1,0:T(8,128)(2,1)} custom-call(bf16[8,2,2,64,512]{4,3,2,1,0:T(8,128)(2,1)S(1)} %bitcast.25, bf16[256,256]{1,0:T(8,128)(2,1)S(1)} %bitcast.26), custom_call_target="tpu_custom_call" | custom-call | tf_op jit(solution)/shard_map/pallas_call | solution.py:313
  (10 shorter events, 0.1 us)

commit v2 on v1

--- a/solution.py
+++ b/solution.py
@@ -12,14 +12,17 @@
 MESH = pl.DeviceIdType.MESH
 
 
-def tables(freq_bins, sample_count):
-    bin_count = freq_bins.shape[0]
+def angles_of(freq_bins, sample_count):
     sample_ids = jnp.arange(sample_count, dtype=jnp.int32)
     phases = freq_bins[:, None] * sample_ids[None, :] % sample_count
     angles = phases.astype(jnp.float32) * (2.0 * math.pi / sample_count)
-    trig_pair = jnp.stack([jnp.cos(angles), -jnp.sin(angles)], axis=1)
+    return jnp.stack([jnp.cos(angles), -jnp.sin(angles)], axis=1)
+
+
+def tables(freq_bins, sample_count):
+    trig_pair = angles_of(freq_bins, sample_count)
     forward = (trig_pair / math.sqrt(sample_count)).astype(jnp.bfloat16)
-    inverse = (trig_pair * math.sqrt(2.0 / bin_count)).astype(jnp.bfloat16)
+    inverse = (trig_pair * math.sqrt(2.0 / freq_bins.shape[0])).astype(jnp.bfloat16)
     return (forward, inverse)
 
 
@@ -34,14 +37,20 @@
     return out.astype(jnp.bfloat16)
 
 
+def spread(trig):
+    count, samples = trig.shape
+    wide = jnp.broadcast_to(trig[:, None, :], (count, SB, samples))
+    return wide.reshape(count * SB, samples).astype(jnp.bfloat16)
+
+
 def row_mod(shape):
     return lax.broadcasted_iota(jnp.int32, shape, 0) % SB
 
 
 def main_kernel(
     n, bins, rows, half, blocks,
-    x_ref, base_ref, gb_ref, back_ref,
-    send, recv, other, full, right, ret,
+    x_ref, trig_ref, miss_ref, neigh_ref, weight_ref, back_ref,
+    send, recv, other, full, right, ret, base_ref, gb_ref,
     send_sem, recv_sem, fsend, frecv, bsend, brecv, lsem,
 ):
     step = pl.program_id(0) * 2 + pl.program_id(1)
@@ -64,7 +73,13 @@
         lax.fori_loop(1, n, greet, 0)
         pl.semaphore_wait(barrier, n - 1)
 
-    mod = row_mod((bins * 2 * SB, x_ref.shape[2]))
+    samples = x_ref.shape[2]
+
+    @pl.when(step == 0)
+    def _():
+        base_ref[...] = spread(trig_ref[...] / math.sqrt(samples))
+
+    mod = row_mod((bins * 2 * SB, samples))
     base = base_ref[...]
     acc = jnp.zeros((bins * 2 * SB, half), jnp.float32)
     for s in range(SB):
@@ -87,7 +102,9 @@
         )
 
     def start_out(d, c):
-        j = (mine + d) % bins
+        hb = bins // 2
+        side = (mine // hb + 1 + d // hb) % 2
+        j = side * hb + (mine + 1 + d) % hb
 
         @pl.when(j * 2 + h != me)
         def _():
@@ -95,7 +112,7 @@
 
         return c
 
-    lax.fori_loop(1, bins + 1, start_out, 0)
+    lax.fori_loop(0, bins, start_out, 0)
 
     @pl.when(h == member)
     def _():
@@ -104,6 +121,31 @@
     @pl.when(step == 2 * blocks - 1)
     def _():
         sibling = mine * 2 + 1 - member
+        miss = miss_ref[...]
+        count = miss.shape[1]
+
+        def band(b, c):
+            first = jnp.minimum(jnp.maximum(2 * b - 1, 0), n - 4) * rows
+            hit = miss == lax.broadcasted_iota(jnp.int32, (2 * rows, count), 0) + b * 2 * rows
+            hit = jnp.where(hit, 1.0, 0.0)
+            kept = 1.0 - jnp.sum(hit, axis=1, keepdims=True)
+            cols = lax.broadcasted_iota(jnp.int32, (count, 4 * rows), 1) + first
+            near = jnp.zeros((count, 4 * rows), jnp.float32)
+            for k in range(neigh_ref.shape[1]):
+                near = near + jnp.where(
+                    neigh_ref[:, k:k + 1] == cols, weight_ref[:, k:k + 1], 0.0
+                )
+            row_id = lax.broadcasted_iota(jnp.int32, (2 * rows, 4 * rows), 0) + b * 2 * rows
+            col_id = lax.broadcasted_iota(jnp.int32, (2 * rows, 4 * rows), 1) + first
+            g = jnp.dot(
+                hit.astype(jnp.bfloat16),
+                near.astype(jnp.bfloat16),
+                preferred_element_type=jnp.float32,
+            ) + jnp.where(row_id == col_id, kept, 0.0)
+            gb_ref[b] = g.astype(jnp.bfloat16)
+            return c
+
+        lax.fori_loop(0, n // 2, band, 0)
 
         def forward(p, sbb):
             a = pl.multiple_of(sbb * SB, SB)
@@ -136,7 +178,7 @@
 
         lax.fori_loop(0, blocks * n, arrive, 0)
 
-        def fill(src, keep):
+        def fill(src, keep, low, high):
             def one(b, c):
                 first = jnp.minimum(jnp.maximum(2 * b - 1, 0), n - 4)
                 g = gb_ref[b]
@@ -147,7 +189,7 @@
                     keep(ch, at_row, val.astype(jnp.bfloat16))
                 return c
 
-            lax.fori_loop(0, n // 2, one, 0)
+            lax.fori_loop(low, high, one, 0)
 
         def keep_own(ch, at_row, val):
             full[ch, member, pl.ds(at_row, 2 * rows), :] = val
@@ -158,14 +200,13 @@
         def keep_other(ch, at_row, val):
             full[ch, 1 - member, pl.ds(at_row, 2 * rows), :] = val
 
-        fill(recv, keep_own)
+        fill(recv, keep_own, 0, n // 2)
 
         def arrived(i, c):
             forward(i % n, i // n).wait()
             return c
 
         lax.fori_loop(0, blocks * n, arrived, 0)
-        fill(other, keep_other)
 
         def back_copy(p):
             return pltpu.make_async_remote_copy(
@@ -183,8 +224,11 @@
         wide = 256
 
         def product(i, c):
-            g = (me // 4 + groups // 2 + i) % groups
+            hg = groups // 2
+            z = me // 4
+            g = (z // hg + 1 + i // hg) % 2 * hg + (z + 1 + i) % hg
             at_row = pl.multiple_of(g * 4 * rows, 4 * rows)
+            fill(other, keep_other, 2 * g, 2 * g + 2)
 
             for col in range(0, half, wide):
                 for ch in range(2):
@@ -250,7 +294,11 @@
         lax.fori_loop(0, n, finish, 0)
 
 
-def inverse_kernel(p_ref, base_ref, o_ref):
+def inverse_kernel(p_ref, trig_ref, o_ref, base_ref):
+    @pl.when((pl.program_id(0) == 0) & (pl.program_id(1) == 0))
+    def _():
+        base_ref[...] = spread(trig_ref[...] * math.sqrt(2.0 / p_ref.shape[0]))
+
     bins, half = p_ref.shape[0], p_ref.shape[-1]
     block = p_ref[...].reshape(bins * 2 * SB, half)
     turned = block.T
@@ -267,16 +315,9 @@
     half = order // 2
     bins = freq_bins.shape[0]
     blocks = rows // SB
-    forward, inverse = tables(freq_bins, samples)
-    forward = jnp.repeat(forward.reshape(2 * bins, samples), SB, axis=0)
-    inverse = jnp.repeat(inverse.reshape(2 * bins, samples), SB, axis=0)
-    b = jnp.arange(n // 2, dtype=jnp.int32)
-    first = jnp.clip(2 * b - 1, 0, n - 4) * rows
+    trig = angles_of(freq_bins, samples).reshape(2 * bins, samples)
+    count = missing.shape[0]
     gshape = (n // 2, 2 * rows, 4 * rows)
-    row_ids = (b[:, None] * 2 * rows + jnp.arange(2 * rows, dtype=jnp.int32)[None, :])[:, :, None]
-    col_ids = (first[:, None] + jnp.arange(4 * rows, dtype=jnp.int32)[None, :])[:, None, :]
-    gb = fill_rows(missing, neighbours, weights, row_ids, col_ids)
-    assert gb.shape == gshape
     cut = bins * 2 * SB
     bf16 = jnp.bfloat16
     dma = pltpu.SemaphoreType.DMA
@@ -286,8 +327,10 @@
         out_shape=jax.ShapeDtypeStruct((n, 2, rows, half), bf16),
         in_specs=[
             pl.BlockSpec((SB, half, samples), lambda i, j: (i, j, 0)),
-            pl.BlockSpec((cut, samples), lambda i, j: (0, 0)),
-            pl.BlockSpec(gshape, lambda i, j: (0, 0, 0)),
+            pl.BlockSpec((2 * bins, samples), lambda i, j: (0, 0)),
+            pl.BlockSpec((1, count), lambda i, j: (0, 0)),
+            pl.BlockSpec(neighbours.shape, lambda i, j: (0, 0)),
+            pl.BlockSpec(weights.shape, lambda i, j: (0, 0)),
         ],
         out_specs=pl.BlockSpec(memory_space=pl.ANY),
         scratch_shapes=[
@@ -297,6 +340,8 @@
             pltpu.VMEM((2, 2, order, half), bf16),
             pltpu.VMEM((3, order, half), bf16),
             pltpu.VMEM((n, 2, rows, half), bf16),
+            pltpu.VMEM((cut, samples), bf16),
+            pltpu.VMEM(gshape, bf16),
             dma((n, blocks)),
             dma((n, blocks)),
             dma((n, blocks)),
@@ -308,7 +353,7 @@
         compiler_params=pltpu.CompilerParams(
             collective_id=0, has_side_effects=True, vmem_limit_bytes=50 * 2**20
         ),
-    )(records, forward, gb)
+    )(records, trig, missing.reshape(1, count), neighbours, weights)
     back = back.reshape(bins, 2, 2, rows, half)
     return pl.pallas_call(
         inverse_kernel,
@@ -316,11 +361,12 @@
         out_shape=jax.ShapeDtypeStruct(records.shape, bf16),
         in_specs=[
             pl.BlockSpec((bins, None, 2, SB, half), lambda i, j: (0, j, 0, i, 0)),
-            pl.BlockSpec((cut, samples), lambda i, j: (0, 0)),
+            pl.BlockSpec((2 * bins, samples), lambda i, j: (0, 0)),
         ],
+        scratch_shapes=[pltpu.VMEM((cut, samples), bf16)],
         out_specs=pl.BlockSpec((SB, half, samples), lambda i, j: (i, j, 0)),
         compiler_params=pltpu.CompilerParams(vmem_limit_bytes=50 * 2**20),
-    )(back, inverse)
+    )(back, trig)
 
 
 def plain(records, missing, neighbours, weights, freq_bins):

time: 130 us -> 128 us (0.985)
  the two profiles are of different devices: /device:TPU:15 before, /device:TPU:7 now
where the time goes in v2:
time: 128 us
  Pallas kernels  125 us (98%)
  local copies, waits for them, and re-layouts  2.25 us (2%)
    pallas_call x1, Pallas kernels, fused(): pl.pallas_call(functools.partial(main_kernel, n, bins, rows, half, blocks...  110 us
    pallas_call x1, Pallas kernels, fused(): pl.pallas_call(inverse_kernel, grid=(blocks, 2), out_shape=jax.ShapeDtype...  14.7 us

profile of v2, /device:TPU:7, one launch (start us, length us, event | category | flops | bytes accessed | tf_op | source)
XLA Modules:
  0.0 127.9 jit_solution(15615639007434191510)
XLA Ops:
  0.0 0.8 fusion.6
  0.8 0.8 copy.9.neigh_ref
  1.6 0.8 copy.10.weight_ref
  2.4 0.0 copy-start
  2.4 0.6 copy-done
  3.1 110.1 %shard_map.55 = bf16[16,2,64,512]{3,2,1,0:T(8,128)(2,1)S(1)} custom-call(bf16[64,1024,256]{2,1,0:T(8,128)(2,1)} %x_ref.1, f32[16,256]{1,0:T(8,128)S(1)} %reshape.103.trig_ref, s32[1,128]{1,0:T(1,128)S(1)} %bitcast.3, s32[128,3]{1,0:T(8,128)S(1)} %copy.9.neigh_ref, f32[128,3]{1,0:T(8,128)S(1)} %copy.10.weight_ref), custom_call_target="tpu_custom_call" | custom-call | tf_op jit(solution)/shard_map/pallas_call | solution.py:324
  113.2 14.7 %shard_map.56 = bf16[64,1024,256]{2,1,0:T(8,128)(2,1)} custom-call(bf16[8,2,2,64,512]{4,3,2,1,0:T(8,128)(2,1)S(1)} %bitcast.2, f32[16,256]{1,0:T(8,128)S(1)} %reshape.103.trig_ref), custom_call_target="tpu_custom_call" | custom-call | tf_op jit(solution)/shard_map/pallas_call | solution.py:358
  (3 shorter events, 0.0 us)
Async XLA Ops:
  2.4 0.7 copy-start

commit v3 on v2

--- a/solution.py
+++ b/solution.py
@@ -102,9 +102,7 @@
         )
 
     def start_out(d, c):
-        hb = bins // 2
-        side = (mine // hb + 1 + d // hb) % 2
-        j = side * hb + (mine + 1 + d) % hb
+        j = (mine + 1 + d) % bins
 
         @pl.when(j * 2 + h != me)
         def _():
@@ -129,17 +127,18 @@
             hit = miss == lax.broadcasted_iota(jnp.int32, (2 * rows, count), 0) + b * 2 * rows
             hit = jnp.where(hit, 1.0, 0.0)
             kept = 1.0 - jnp.sum(hit, axis=1, keepdims=True)
-            cols = lax.broadcasted_iota(jnp.int32, (count, 4 * rows), 1) + first
-            near = jnp.zeros((count, 4 * rows), jnp.float32)
-            for k in range(neigh_ref.shape[1]):
+            cols = lax.broadcasted_iota(jnp.int32, (4 * rows, count), 0) + first
+            near = jnp.zeros((4 * rows, count), jnp.float32)
+            for k in range(neigh_ref.shape[0]):
                 near = near + jnp.where(
-                    neigh_ref[:, k:k + 1] == cols, weight_ref[:, k:k + 1], 0.0
+                    neigh_ref[k:k + 1, :] == cols, weight_ref[k:k + 1, :], 0.0
                 )
             row_id = lax.broadcasted_iota(jnp.int32, (2 * rows, 4 * rows), 0) + b * 2 * rows
             col_id = lax.broadcasted_iota(jnp.int32, (2 * rows, 4 * rows), 1) + first
-            g = jnp.dot(
+            g = lax.dot_general(
                 hit.astype(jnp.bfloat16),
                 near.astype(jnp.bfloat16),
+                (((1,), (1,)), ((), ())),
                 preferred_element_type=jnp.float32,
             ) + jnp.where(row_id == col_id, kept, 0.0)
             gb_ref[b] = g.astype(jnp.bfloat16)
@@ -224,9 +223,7 @@
         wide = 256
 
         def product(i, c):
-            hg = groups // 2
-            z = me // 4
-            g = (z // hg + 1 + i // hg) % 2 * hg + (z + 1 + i) % hg
+            g = (me // 4 + groups // 2 + i) % groups
             at_row = pl.multiple_of(g * 4 * rows, 4 * rows)
             fill(other, keep_other, 2 * g, 2 * g + 2)
 
@@ -329,8 +326,8 @@
             pl.BlockSpec((SB, half, samples), lambda i, j: (i, j, 0)),
             pl.BlockSpec((2 * bins, samples), lambda i, j: (0, 0)),
             pl.BlockSpec((1, count), lambda i, j: (0, 0)),
-            pl.BlockSpec(neighbours.shape, lambda i, j: (0, 0)),
-            pl.BlockSpec(weights.shape, lambda i, j: (0, 0)),
+            pl.BlockSpec(neighbours.shape[::-1], lambda i, j: (0, 0)),
+            pl.BlockSpec(weights.shape[::-1], lambda i, j: (0, 0)),
         ],
         out_specs=pl.BlockSpec(memory_space=pl.ANY),
         scratch_shapes=[
@@ -353,7 +350,7 @@
         compiler_params=pltpu.CompilerParams(
             collective_id=0, has_side_effects=True, vmem_limit_bytes=50 * 2**20
         ),
-    )(records, trig, missing.reshape(1, count), neighbours, weights)
+    )(records, trig, missing.reshape(1, count), neighbours.T, weights.T)
     back = back.reshape(bins, 2, 2, rows, half)
     return pl.pallas_call(
         inverse_kernel,

time: 128 us -> 124 us (0.969)
  the two profiles are of different devices: /device:TPU:7 before, /device:TPU:15 now
where the time goes in v3:
time: 124 us; the launch traced here: 123 us
  Pallas kernels  120 us (97%)
  local copies, waits for them, and re-layouts  2.04 us (2%)
    pallas_call x1, Pallas kernels, fused(): pl.pallas_call(functools.partial(main_kernel, n, bins, rows, half, blocks...  106 us
    pallas_call x1, Pallas kernels, fused(): pl.pallas_call(inverse_kernel, grid=(blocks, 2), out_shape=jax.ShapeDtype...  14.7 us

profile of v3, /device:TPU:15, one launch (start us, length us, event | category | flops | bytes accessed | tf_op | source)
XLA Modules:
  0.0 123.3 jit_solution(3538411326836583824)
XLA Ops:
  0.0 0.8 fusion.6
  0.8 0.0 copy-start
  0.8 0.7 copy-done
  1.5 0.0 copy-start.1
  1.5 0.7 copy-done.1
  2.2 0.0 copy-start.2
  2.2 0.7 copy-done.2
  2.9 105.7 %shard_map.55 = bf16[16,2,64,512]{3,2,1,0:T(8,128)(2,1)S(1)} custom-call(bf16[64,1024,256]{2,1,0:T(8,128)(2,1)} %x_ref.1, f32[16,256]{1,0:T(8,128)S(1)} %reshape.103.trig_ref, s32[1,128]{1,0:T(1,128)S(1)} %bitcast.7, s32[3,128]{1,0:T(4,128)S(1)} %bitcast.5, f32[3,128]{1,0:T(4,128)S(1)} %bitcast.6), custom_call_target="tpu_custom_call" | custom-call | tf_op jit(solution)/shard_map/pallas_call | solution.py:321
  108.6 14.7 %shard_map.56 = bf16[64,1024,256]{2,1,0:T(8,128)(2,1)} custom-call(bf16[8,2,2,64,512]{4,3,2,1,0:T(8,128)(2,1)S(1)} %bitcast.4, f32[16,256]{1,0:T(8,128)S(1)} %reshape.103.trig_ref), custom_call_target="tpu_custom_call" | custom-call | tf_op jit(solution)/shard_map/pallas_call | solution.py:355
  (3 shorter events, 0.0 us)
Async XLA Ops:
  0.8 0.7 copy-start
  1.5 0.7 copy-start.1
  2.2 0.7 copy-start.2
